TPU v7x, 512 devices: a whole 4x8x8 slice. The times are simulated.
512 devices in a mesh: wide: 32 (over y, x), narrow: 16 (over z, core).
Axes of the slice: x: 4, y: 8, z: 8, core: 2. Of those that a mesh axis runs over, the one named last changes fastest.
Arguments:
- hamiltonian: float32 [1024, 3, 128, 128], P(('wide', 'narrow')), may hold values from -3.3 to 3.3, as said below
- old_density: float32 [1024, 3, 128, 128], P(('wide', 'narrow')), may hold values from -2 to 2
- neighbours: int32 [1024, 3], P(('wide', 'narrow')), may hold values from 0 to 31, as said below
- live: int32 [1024], P(('wide', 'narrow')), may hold values from 0 to 1, as said below
- potential: float32 [1], replicated, may hold values from -1 to 1
Outputs:
- density: float32 [1024, 3, 128, 128], P(('wide', 'narrow'))
Inputs may be any that keep to these rules, and one draw needn't show every extreme that they name: Within each cluster of 32 consecutive blocks, entry 0 is the block's own index in the cluster and entries 1 and 2 are its neighbours on a cycle through all blocks of the cluster: block a is entry 1 of its entry-2 neighbour and entry 2 of its entry-1 neighbour. Along the cycle the 2 blocks of one device stand next to each other in some order; the devices of the narrow axis follow each other in an order drawn from the seed. For each index of the narrow axis, the devices at wide indices i and i + 16 own at most 2 live blocks together; in every draw some device owns 2 live blocks. `hamiltonian`: the block Hamiltonian is symmetric: tile 1 of block c is the transpose of tile 2 of prev(c), and tile 0 is symmetric.
All inputs are finite; a program needn't handle non-finite values. Where the computation divides by a largest or mean magnitude, that divisor is 1e-20 or more.
Results may differ from a plain program's by a relative error of at most 0.0001.
Values sent between devices are 32-bit elements; how exact they have to be, the bound alone decides.
A program may use at most 64 MiB of HBM per device.

v0:
```python
import jax
import jax.numpy as jnp
from jax import lax
from jax.sharding import PartitionSpec as P

ITERS = 4
epsilon = 1e-06


def in_one_piece(arrays, axis, dim, along):
    widths = [a.shape[along] for a in arrays]
    both = jnp.concatenate(arrays, axis=along)
    out = lax.all_gather(both, axis, axis=dim, tiled=True)
    return tuple(jnp.split(out, [sum(widths[:k]) for k in range(1, len(widths))], axis=along))


def product(left, right):
    return jnp.matmul(left, right, precision=lax.Precision.HIGHEST)


def transpose_tiles(tiles):
    return jnp.swapaxes(tiles, -1, -2)


def assemble(row_tiles, prev_onsite, next_onsite, level):
    zero_tile = jnp.zeros_like(prev_onsite)
    upper_rows = jnp.concatenate(
        [row_tiles[..., 0, :, :], row_tiles[..., 1, :, :], row_tiles[..., 2, :, :]], axis=-1
    )
    middle_rows = jnp.concatenate(
        [transpose_tiles(row_tiles[..., 1, :, :]), prev_onsite, zero_tile], axis=-1
    )
    lower_rows = jnp.concatenate(
        [transpose_tiles(row_tiles[..., 2, :, :]), zero_tile, next_onsite], axis=-1
    )
    matrix = jnp.concatenate([upper_rows, middle_rows, lower_rows], axis=-2)
    order = matrix.shape[-1]
    return matrix - level * jnp.eye(order, dtype=jnp.float32)


def sign_columns(matrix, width, depth):
    order = matrix.shape[-1]
    identity = jnp.eye(order, dtype=jnp.float32)
    bound = jnp.max(jnp.sum(jnp.abs(matrix), axis=-1), axis=-1) + epsilon
    current = matrix / bound[..., None, None]
    for sweep in range(depth - 1):
        square = product(current, current)
        current = 0.5 * product(current, 3.0 * identity - square)
    square = product(current, current)
    final_cols = 0.5 * product(current, 3.0 * identity[:, :width] - square[..., :, :width])
    columns = 0.5 * (identity[:, :width] - final_cols)
    return columns.reshape(columns.shape[:-2] + (order // width, width, width))


def shards(hamiltonian, old_density, neighbours, live, potential):
    width = hamiltonian.shape[-1]
    level = potential[0]
    cluster_onsite = lax.all_gather(hamiltonian[:, 0], "narrow", axis=0, tiled=True)
    prev_onsite = jnp.take(cluster_onsite, neighbours[:, 1], axis=0)
    next_onsite = jnp.take(cluster_onsite, neighbours[:, 2], axis=0)
    matrices = assemble(hamiltonian, prev_onsite, next_onsite, level)
    new_cols = sign_columns(matrices, width, ITERS)
    fresh_cols = jnp.where(live[:, None, None, None] == 1, new_cols, old_density)
    prev_side, next_side = in_one_piece((fresh_cols[:, 1], fresh_cols[:, 2]), "narrow", 0, 1)
    from_prev = jnp.take(next_side, neighbours[:, 1], axis=0)
    from_next = jnp.take(prev_side, neighbours[:, 2], axis=0)
    return jnp.stack(
        [
            0.5 * (fresh_cols[:, 0] + transpose_tiles(fresh_cols[:, 0])),
            0.5 * (fresh_cols[:, 1] + transpose_tiles(from_prev)),
            0.5 * (fresh_cols[:, 2] + transpose_tiles(from_next)),
        ],
        axis=1,
    )


def solution(mesh):
    placed = (
        P(("wide", "narrow"), None, None, None),
        P(("wide", "narrow"), None, None, None),
        P(("wide", "narrow"), None),
        P(("wide", "narrow")),
        P(),
    )
    return jax.shard_map(
        shards,
        mesh=mesh,
        in_specs=placed,
        out_specs=P(("wide", "narrow"), None, None, None),
        check_vma=False,
    )
```

profile of v0, /device:TPU:1, one launch (start us, length us, event | category | flops | bytes accessed | tf_op | source)
XLA Modules:
  0.0 140.7 jit_solution(15930580519983071181)
XLA Ops:
  6.5 0.0 copy-start.1
  6.5 0.0 all-gather.6.cloned.1.call-start
  6.5 1.8 %slice_bitcast_fusion.5 = (f32[2,128,128]{2,1,0:T(8,128)S(1)}, f32[2,128,128]{2,1,0:T(8,128)S(1)}, f32[2,128,128]{2,1,0:T(8,128)S(1)}, f32[2,1,128,128]{3,2,1,0:...) fusion(f32[2,3,128,128]{3,2,1,0:T(8,128)} %param.7), kind=kLoop, calls=%fused_computation.51 | loop fusion | bytes 1179648 | tf_op jit(solution)/shard_map/squeeze | solution.py:28
  8.3 0.0 copy-start.2
  8.3 0.0 all-gather.6.cloned.1.call-update
  8.3 0.0 all-gather.4.cloned.1.call-start
  9.0 0.1 copy.68
  9.1 0.1 copy.69
  9.2 0.0 copy-done.1
  9.2 0.2 slice_reduce_fusion.1
  9.6 0.0 copy-done.2
  9.7 48.9 %all-gather.6.cloned.1.call-done = f32[32,1,128,128]{3,2,1,0:T(8,128)} async-done(((f32[2,1,128,128]{3,2,1,0:T(8,128)}), f32[32,1,128,128]{3,2,1,0:T(8,128)}) %all-gather.6.cloned.1.call-update) | async-done | bytes 2097168 | tf_op jit(solution)/shard_map/all_gather | solution.py:58
  58.6 2.1 %gather_fusion.1 = f32[2,128,128]{2,1,0:T(8,128)S(1)} fusion(f32[32,128,128]{2,1,0:T(8,128)} %bitcast.68, s32[1024]{0:T(1024)S(1)} %pad_clamp_fusion), kind=kCustom, calls=%fused_computation.1.clone | custom fusion | bytes 262152 | tf_op jit(solution)/shard_map/jit(_take)/gather | solution.py:60
  60.8 2.1 %gather_fusion = f32[2,128,128]{2,1,0:T(8,128)S(1)} fusion(f32[32,128,128]{2,1,0:T(8,128)} %bitcast.69, s32[1024]{0:T(1024)S(1)} %pad_clamp_fusion.1), kind=kCustom, calls=%fused_computation.clone | custom fusion | bytes 262152 | tf_op jit(solution)/shard_map/jit(_take)/gather | solution.py:59
  62.9 0.1 broadcast_select_fusion.1
  63.0 0.1 broadcast_select_fusion
  63.1 0.2 abs_reduce_fusion
  63.3 0.1 reduce_max.9
  63.5 2.6 %convolution_subtract_fusion.2 = f32[2,384,384]{2,1,0:T(8,128)S(1)} fusion(f32[384,384]{1,0:T(8,128)S(1)} %fusion.3, f32[2]{0:T(128)S(1)} %broadcast_add_fusion, f32[2,128,128]{2,1,0:T(8,128)S(1)} %broadcast_select_fusion, f32[2,128,128]{2,1,0:T(8,128)S(1)} %broadcast_in_dim.17, f32[2,128,128]{2,1,0:T(8,128)S(1)} %bitcast.66, ...), kind=kOutput, calls=%fused_computation.9 | convolution fusion | flops 1362198528 | bytes 3407880 | tf_op jit(solution)/shard_map/dot_general | solution.py:18
  66.1 2.5 %convolution_multiply_fusion.2 = f32[2,384,384]{2,1,0:T(8,128)S(1)} fusion(f32[2,384,384]{2,1,0:T(8,128)S(1)} %convolution_subtract_fusion.2, f32[2]{0:T(128)S(1)} %broadcast_add_fusion, f32[2,128,128]{2,1,0:T(8,128)S(1)} %broadcast_select_fusion, f32[2,128,128]{2,1,0:T(8,128)S(1)} %broadcast_in_dim.17, f32[2,128,128]{2,1,0:T(8,128)S(1)} %bitcast.67, ...), kind=kOutput, calls=%fused_computation.8 | convolution fusion | flops 1362198528 | bytes 3997704 | tf_op jit(solution)/shard_map/dot_general | solution.py:18
  68.6 2.5 %convolution_subtract_fusion.1 = f32[2,384,384]{2,1,0:T(8,128)S(1)} fusion(f32[2,384,384]{2,1,0:T(8,128)S(1)} %convolution_multiply_fusion.2, f32[384,384]{1,0:T(8,128)S(1)} %fusion.3), kind=kOutput, calls=%fused_computation.7 | convolution fusion | flops 1359249408 | bytes 2949120 | tf_op jit(solution)/shard_map/dot_general | solution.py:18
  71.1 2.4 %convolution_multiply_fusion.1 = f32[2,384,384]{2,1,0:T(8,128)S(1)} fusion(f32[2,384,384]{2,1,0:T(8,128)S(1)} %convolution_multiply_fusion.2, f32[2,384,384]{2,1,0:T(8,128)S(1)} %convolution_subtract_fusion.1), kind=kOutput, calls=%fused_computation.6 | convolution fusion | flops 1359249408 | bytes 3538944 | tf_op jit(solution)/shard_map/dot_general | solution.py:18
  73.5 2.7 %convolution_subtract_fusion = f32[2,384,384]{2,1,0:T(8,128)S(1)} fusion(f32[2,384,384]{2,1,0:T(8,128)S(1)} %convolution_multiply_fusion.1, f32[384,384]{1,0:T(8,128)S(1)} %fusion.3), kind=kOutput, calls=%fused_computation.5 | convolution fusion | flops 1359249408 | bytes 2949120 | tf_op jit(solution)/shard_map/dot_general | solution.py:18
  76.2 2.4 %convolution_multiply_fusion = f32[2,384,384]{2,1,0:T(8,128)S(1)} fusion(f32[2,384,384]{2,1,0:T(8,128)S(1)} %convolution_multiply_fusion.1, f32[2,384,384]{2,1,0:T(8,128)S(1)} %convolution_subtract_fusion), kind=kOutput, calls=%fused_computation.4 | convolution fusion | flops 1359249408 | bytes 3538944 | tf_op jit(solution)/shard_map/dot_general | solution.py:18
  78.7 1.2 convolution_subtract_fusion.3
  79.8 0.0 copy-start
  79.9 1.2 fusion.1
  81.0 0.0 copy-done
  81.1 0.1 copy_select_fusion
  81.2 0.7 pad_maximum_fusion.1
  81.9 0.0 all-gather.4.cloned.1.call-update
  81.9 0.1 copy.63
  82.0 0.1 copy.62
  82.2 43.7 %all-gather.4.cloned.1.call-done = f32[32,256,128]{2,1,0:T(8,128)} async-done(((f32[2,256,128]{2,1,0:T(8,128)}), f32[32,256,128]{2,1,0:T(8,128)}) %all-gather.4.cloned.1.call-update) | async-done | bytes 4194320 | tf_op jit(solution)/shard_map/all_gather | solution.py:13
  125.9 3.9 %fusion.9 = (f32[32,128,128]{2,1,0:T(8,128)}, f32[32,128,128]{2,1,0:T(8,128)S(1)}) fusion(f32[32,256,128]{2,1,0:T(8,128)} %all-gather.4.cloned.1.call-done), kind=kLoop, calls=%fused_computation.52 | loop fusion | bytes 8388608 | tf_op jit(solution)/shard_map/split | solution.py:14
  129.8 2.1 %gather_fusion.2 = f32[2,128,128]{2,1,0:T(8,128)S(1)} fusion(f32[32,128,128]{2,1,0:T(8,128)} %get-tuple-element.8, s32[1024]{0:T(1024)S(1)} %pad_clamp_fusion.1), kind=kCustom, calls=%fused_computation.2.clone | custom fusion | bytes 262152 | tf_op jit(solution)/shard_map/jit(_take)/gather | solution.py:65
  131.9 0.6 gather_fusion.3
  132.5 0.1 copy.64
  132.6 0.1 bitcast_add_fusion.1
  132.7 0.1 copy.65
  132.8 0.1 fusion.8
  132.9 0.9 copy.66
  (16 shorter events, 0.3 us)
Async XLA Ops:
  6.5 2.7 %copy-start.1 = (s32[2,3]{1,0:T(2,128)S(1)}, s32[2,3]{1,0:T(2,128)}, u32[]{:S(2)}) copy-start(s32[2,3]{1,0:T(2,128)} %param.9) | copy-start | bytes 76
  6.5 52.1 %all-gather.6.cloned.1.call-start = ((), (), s32[]{:S(2)}) async-start(), calls=%async_computation.1 | async-start | bytes 2228224 | tf_op jit(solution)/shard_map/all_gather | solution.py:58
  8.3 1.3 copy-start.2
  8.3 117.5 %all-gather.4.cloned.1.call-start = ((), (), s32[]{:S(2)}) async-start(), calls=%async_computation | async-start | bytes 4456448 | tf_op jit(solution)/shard_map/all_gather | solution.py:13
  79.8 1.2 copy-start
Sparse Core Ops, SparseCore 0:
  9.5 49.0 all-gather.5
  82.1 43.7 all-gather.3
where the time goes:
time: 141 us
  waiting for transfers between devices  92.6 us (66%)
  matrix products  17.5 us (12%)
  local copies, waits for them, and re-layouts  14.4 us (10%)
  between operations  14.3 us (10%)
  other arithmetic  1.79 us (1%)
    all_gather x1, waiting for transfers between devices, shards(): lax.all_gather(hamiltonian[:, 0], 'narrow', axis=0, tiled=True)  48.9 us
    all_gather x1, waiting for transfers between devices, in_one_piece(): out = lax.all_gather(both, axis, axis=dim, tiled=True)  43.7 us
    dot_general x8, matrix products, product(): return jnp.matmul(left, right, precision=lax.Precision.HIGHEST)  17.5 us
    split x1, local copies, waits for them, and re-layouts, in_one_piece(): jnp.split(out, [sum(widths[:k]) for k in range(1, len(widths))], axis=along)  3.92 us
  transfers between devices with their start and end apart: 2, of which 2 were waited for; matrix products, arithmetic and copies ran while one was open for 1% of the time, Pallas kernels for 0%

commit v1 on v0

--- a/solution.py
+++ b/solution.py
@@ -55,7 +55,16 @@
 def shards(hamiltonian, old_density, neighbours, live, potential):
     width = hamiltonian.shape[-1]
     level = potential[0]
-    cluster_onsite = lax.all_gather(hamiltonian[:, 0], "narrow", axis=0, tiled=True)
+    x = hamiltonian[:, 0]
+    ways, here, lap = (lax.axis_size("narrow"), lax.axis_index("narrow"), x.shape[0])
+    line, have = (x, 1)
+    while have < ways:
+        line = jnp.concatenate(
+            [line, lax.ppermute(line, "narrow", [(d, (d - have) % ways) for d in range(ways)])],
+            axis=0,
+        )
+        have = 2 * have
+    cluster_onsite = jnp.roll(line, here * lap, axis=0)
     prev_onsite = jnp.take(cluster_onsite, neighbours[:, 1], axis=0)
     next_onsite = jnp.take(cluster_onsite, neighbours[:, 2], axis=0)
     matrices = assemble(hamiltonian, prev_onsite, next_onsite, level)

time: 141 us -> 193 us (1.37)
  waiting for transfers between devices: 92.6 us -> 119 us
  starting transfers between devices: 0.04 us -> 21.5 us
  other arithmetic: 1.79 us -> 6.16 us
    ppermute x0 -> x4, waiting for transfers between devices: none -> 72.5 us  [shards(): lax.ppermute(line, 'narrow', [(d, (d - have) % ways) for d in range(ways)])]
    all_gather x1 -> x0, waiting for transfers between devices: 48.9 us -> none  [shards(): lax.all_gather(hamiltonian[:, 0], 'narrow', axis=0, tiled=True)]
    ppermute x0 -> x4, starting transfers between devices: none -> 21.5 us  [shards(): lax.ppermute(line, 'narrow', [(d, (d - have) % ways) for d in range(ways)])]
    all_gather x1, waiting for transfers between devices: 43.7 us -> 46.8 us  [in_one_piece(): out = lax.all_gather(both, axis, axis=dim, tiled=True)]
  transfers between devices with their start and end apart: 2 -> 5, of which waited for: 2 -> 4; matrix products, arithmetic and copies ran while one was open for 1% -> 3% of each run, Pallas kernels for 0% -> 0%
where the time goes in v1:
time: 193 us
  waiting for transfers between devices  119 us (62%)
  starting transfers between devices  21.5 us (11%)
  matrix products  17.5 us (9%)
  between operations  14.5 us (8%)
  local copies, waits for them, and re-layouts  13.5 us (7%)
  other arithmetic  6.16 us (3%)
    ppermute x4, waiting for transfers between devices, shards(): lax.ppermute(line, 'narrow', [(d, (d - have) % ways) for d in range(ways)])  72.5 us
    all_gather x1, waiting for transfers between devices, in_one_piece(): out = lax.all_gather(both, axis, axis=dim, tiled=True)  46.8 us
    ppermute x4, starting transfers between devices, shards(): lax.ppermute(line, 'narrow', [(d, (d - have) % ways) for d in range(ways)])  21.5 us
    dot_general x8, matrix products, product(): return jnp.matmul(left, right, precision=lax.Precision.HIGHEST)  17.5 us
    split x1, local copies, waits for them, and re-layouts, in_one_piece(): jnp.split(out, [sum(widths[:k]) for k in range(1, len(widths))], axis=along)  3.93 us
  transfers between devices with their start and end apart: 5, of which 4 were waited for; matrix products, arithmetic and copies ran while one was open for 3% of the time, Pallas kernels for 0%

profile of v1, /device:TPU:1, one launch (start us, length us, event | category | flops | bytes accessed | tf_op | source)
XLA Modules:
  0.0 192.6 jit_solution(14416583748730691695)
XLA Ops:
  6.5 1.1 fusion.10
  7.6 6.9 %collective-permute-start = (f32[2,128,128]{2,1,0:T(8,128)S(1)}, f32[2,128,128]{2,1,0:T(8,128)S(1)}, u32[]{:S(2)}, u32[]{:S(2)}) collective-permute-start(f32[2,128,128]{2,1,0:T(8,128)S(1)} %get-tuple-element.14), channel_id=1, source_target_pairs={{0,15},{1,0},{2,1},{3,2},{4,3},{5,4},{6,5},{7,6},{8,7},{9,8},{10,9... | collective-permute-start | bytes 393224 | tf_op jit(solution)/shard_map/ppermute | solution.py:63
  14.5 1.0 slice_reduce_fusion.1
  15.5 0.1 copy.53
  15.6 0.1 copy.62
  15.7 0.1 copy.63
  15.9 8.9 %collective-permute-start.1 = (f32[4,128,128]{2,1,0:T(8,128)S(1)}, f32[4,128,128]{2,1,0:T(8,128)S(1)}, u32[]{:S(2)}, u32[]{:S(2)}) collective-permute-start(f32[4,128,128]{2,1,0:T(8,128)S(1)} %pad_maximum_fusion.4), channel_id=1, source_target_pairs={{0,14},{1,15},{2,0},{3,1},{4,2},{5,3},{6,4},{7,5},{8,6},{9,7},{10,... | collective-permute-start | bytes 786440 | tf_op jit(solution)/shard_map/ppermute | solution.py:63
  24.8 0.9 copy.54
  26.4 0.9 fusion.3
  27.3 1.6 collective-permute-done.1
  28.9 3.8 %collective-permute-start.2 = (f32[8,128,128]{2,1,0:T(8,128)S(1)}, f32[8,128,128]{2,1,0:T(8,128)S(1)}, u32[]{:S(2)}, u32[]{:S(2)}) collective-permute-start(f32[8,128,128]{2,1,0:T(8,128)S(1)} %pad_maximum_fusion.1), channel_id=1, source_target_pairs={{0,12},{1,13},{2,14},{3,15},{4,0},{5,1},{6,2},{7,3},{8,4},{9,5},{1... | collective-permute-start | bytes 1572872 | tf_op jit(solution)/shard_map/ppermute | solution.py:63
  32.8 22.7 %collective-permute-done.2 = f32[8,128,128]{2,1,0:T(8,128)S(1)} collective-permute-done((f32[8,128,128]{2,1,0:T(8,128)S(1)}, f32[8,128,128]{2,1,0:T(8,128)S(1)}, u32[]{:S(2)}, u32[]{:S(2)}) %collective-permute-start.2) | collective-permute-done | bytes 524320 | tf_op jit(solution)/shard_map/ppermute | solution.py:63
  55.5 0.1 pad_maximum_fusion
  55.6 1.9 collective-permute-start.3
  57.6 0.7 slice_select_fusion
  58.3 0.7 slice_convert_fusion
  59.1 48.2 %collective-permute-done.3 = f32[16,128,128]{2,1,0:T(8,128)S(1)} collective-permute-done((f32[16,128,128]{2,1,0:T(8,128)S(1)}, f32[16,128,128]{2,1,0:T(8,128)S(1)}, u32[]{:S(2)}, u32[]{:S(2)}) %collective-permute-start.3) | collective-permute-done | bytes 1048608 | tf_op jit(solution)/shard_map/ppermute | solution.py:63
  107.3 0.1 constant_dynamic-update-slice_fusion.5
  107.5 0.1 constant_dynamic-update-slice_fusion
  107.5 0.2 constant_dynamic-slice_fusion
  107.8 1.2 gather_fusion
  109.0 0.6 gather_fusion.1
  109.6 1.0 broadcast_select_fusion.1
  110.6 0.1 broadcast_select_fusion
  110.7 1.3 abs_reduce_fusion
  112.0 0.1 reduce_max.9
  112.2 2.6 %convolution_subtract_fusion.2 = f32[2,384,384]{2,1,0:T(8,128)S(1)} fusion(f32[384,384]{1,0:T(8,128)S(1)} %get-tuple-element.20, f32[2]{0:T(128)S(1)} %broadcast_add_fusion, f32[2,128,128]{2,1,0:T(8,128)S(1)} %broadcast_select_fusion, f32[2,128,128]{2,1,0:T(8,128)S(1)} %broadcast_in_dim.17, f32[2,128,128]{2,1,0:T(8,128)S(1)} %bitcast.63, ...), kind=kOutput, calls=%fused_computation.9 | convolution fusion | flops 1361608704 | bytes 3407880 | tf_op jit(solution)/shard_map/dot_general | solution.py:18
  114.8 2.5 %convolution_multiply_fusion.2 = f32[2,384,384]{2,1,0:T(8,128)S(1)} fusion(f32[2,384,384]{2,1,0:T(8,128)S(1)} %convolution_subtract_fusion.2, f32[2]{0:T(128)S(1)} %broadcast_add_fusion, f32[2,128,128]{2,1,0:T(8,128)S(1)} %broadcast_select_fusion, f32[2,128,128]{2,1,0:T(8,128)S(1)} %broadcast_in_dim.17, f32[2,128,128]{2,1,0:T(8,128)S(1)} %bitcast.64, ...), kind=kOutput, calls=%fused_computation.8 | convolution fusion | flops 1361608704 | bytes 3997704 | tf_op jit(solution)/shard_map/dot_general | solution.py:18
  117.3 2.5 %convolution_subtract_fusion.1 = f32[2,384,384]{2,1,0:T(8,128)S(1)} fusion(f32[2,384,384]{2,1,0:T(8,128)S(1)} %convolution_multiply_fusion.2, f32[384,384]{1,0:T(8,128)S(1)} %get-tuple-element.20), kind=kOutput, calls=%fused_computation.7 | convolution fusion | flops 1359249408 | bytes 2949120 | tf_op jit(solution)/shard_map/dot_general | solution.py:18
  119.8 2.4 %convolution_multiply_fusion.1 = f32[2,384,384]{2,1,0:T(8,128)S(1)} fusion(f32[2,384,384]{2,1,0:T(8,128)S(1)} %convolution_multiply_fusion.2, f32[2,384,384]{2,1,0:T(8,128)S(1)} %convolution_subtract_fusion.1), kind=kOutput, calls=%fused_computation.6 | convolution fusion | flops 1359249408 | bytes 3538944 | tf_op jit(solution)/shard_map/dot_general | solution.py:18
  122.2 2.7 %convolution_subtract_fusion = f32[2,384,384]{2,1,0:T(8,128)S(1)} fusion(f32[2,384,384]{2,1,0:T(8,128)S(1)} %convolution_multiply_fusion.1, f32[384,384]{1,0:T(8,128)S(1)} %get-tuple-element.20), kind=kOutput, calls=%fused_computation.5 | convolution fusion | flops 1359249408 | bytes 2949120 | tf_op jit(solution)/shard_map/dot_general | solution.py:18
  124.9 2.4 %convolution_multiply_fusion = f32[2,384,384]{2,1,0:T(8,128)S(1)} fusion(f32[2,384,384]{2,1,0:T(8,128)S(1)} %convolution_multiply_fusion.1, f32[2,384,384]{2,1,0:T(8,128)S(1)} %convolution_subtract_fusion), kind=kOutput, calls=%fused_computation.4 | convolution fusion | flops 1359249408 | bytes 3538944 | tf_op jit(solution)/shard_map/dot_general | solution.py:18
  127.4 1.2 convolution_subtract_fusion.3
  128.6 1.2 fusion.1
  129.8 0.1 copy_select_fusion
  129.9 0.7 pad_maximum_fusion.5
  130.7 0.0 all-gather.2.cloned.1.call-update
  130.7 0.1 copy.58
  130.8 0.1 copy.57
  130.9 46.8 %all-gather.2.cloned.1.call-done = f32[32,256,128]{2,1,0:T(8,128)} async-done(((f32[2,256,128]{2,1,0:T(8,128)}), f32[32,256,128]{2,1,0:T(8,128)}) %all-gather.2.cloned.1.call-update) | async-done | bytes 4194320 | tf_op jit(solution)/shard_map/all_gather | solution.py:13
  177.7 3.9 %fusion.9 = (f32[32,128,128]{2,1,0:T(8,128)}, f32[32,128,128]{2,1,0:T(8,128)S(1)}) fusion(f32[32,256,128]{2,1,0:T(8,128)} %all-gather.2.cloned.1.call-done), kind=kLoop, calls=%fused_computation.65 | loop fusion | bytes 8388608 | tf_op jit(solution)/shard_map/split | solution.py:14
  181.6 2.1 %gather_fusion.2 = f32[2,128,128]{2,1,0:T(8,128)S(1)} fusion(f32[32,128,128]{2,1,0:T(8,128)} %get-tuple-element.8, s32[1024]{0:T(1024)S(1)} %pad_clamp_fusion.1), kind=kCustom, calls=%fused_computation.2.clone | custom fusion | bytes 262152 | tf_op jit(solution)/shard_map/jit(_take)/gather | solution.py:74
  183.8 0.6 gather_fusion.3
  184.4 0.1 copy.59
  184.5 0.1 bitcast_add_fusion.1
  184.6 0.1 copy.60
  184.7 0.1 fusion.8
  184.8 0.9 copy.61
  (39 shorter events, 0.5 us)
Async XLA Ops:
  6.5 171.2 %all-gather.2.cloned.1.call-start = ((), (), s32[]{:S(2)}) async-start(), calls=%async_computation | async-start | bytes 4456448 | tf_op jit(solution)/shard_map/all_gather | solution.py:13
  7.6 8.2 %collective-permute-start = (f32[2,128,128]{2,1,0:T(8,128)S(1)}, f32[2,128,128]{2,1,0:T(8,128)S(1)}, u32[]{:S(2)}, u32[]{:S(2)}) collective-permute-start(f32[2,128,128]{2,1,0:T(8,128)S(1)} %get-tuple-element.14), channel_id=1, source_target_pairs={{0,15},{1,0},{2,1},{3,2},{4,3},{5,4},{6,5},{7,6},{8,7},{9,8},{10,9... | collective-permute-start | bytes 393224 | tf_op jit(solution)/shard_map/ppermute | solution.py:63
  15.9 13.1 %collective-permute-start.1 = (f32[4,128,128]{2,1,0:T(8,128)S(1)}, f32[4,128,128]{2,1,0:T(8,128)S(1)}, u32[]{:S(2)}, u32[]{:S(2)}) collective-permute-start(f32[4,128,128]{2,1,0:T(8,128)S(1)} %pad_maximum_fusion.4), channel_id=1, source_target_pairs={{0,14},{1,15},{2,0},{3,1},{4,2},{5,3},{6,4},{7,5},{8,6},{9,7},{10,... | collective-permute-start | bytes 786440 | tf_op jit(solution)/shard_map/ppermute | solution.py:63
  26.3 6.4 %copy-start.6 = (s32[2]{0:T(128)S(1)}, s32[2]{0:T(128)}, u32[]{:S(2)}) copy-start(s32[2]{0:T(128)} %param.10) | copy-start | bytes 28
  28.9 26.6 %collective-permute-start.2 = (f32[8,128,128]{2,1,0:T(8,128)S(1)}, f32[8,128,128]{2,1,0:T(8,128)S(1)}, u32[]{:S(2)}, u32[]{:S(2)}) collective-permute-start(f32[8,128,128]{2,1,0:T(8,128)S(1)} %pad_maximum_fusion.1), channel_id=1, source_target_pairs={{0,12},{1,13},{2,14},{3,15},{4,0},{5,1},{6,2},{7,3},{8,4},{9,5},{1... | collective-permute-start | bytes 1572872 | tf_op jit(solution)/shard_map/ppermute | solution.py:63
  32.8 26.2 %copy-start.2 = (f32[2,3,128,128]{3,2,1,0:T(8,128)S(1)}, f32[2,3,128,128]{3,2,1,0:T(8,128)}, u32[]{:S(2)}) copy-start(f32[2,3,128,128]{3,2,1,0:T(8,128)} %param.7) | copy-start | bytes 1179652
  55.6 51.6 %collective-permute-start.3 = (f32[16,128,128]{2,1,0:T(8,128)S(1)}, f32[16,128,128]{2,1,0:T(8,128)S(1)}, u32[]{:S(2)}, u32[]{:S(2)}) collective-permute-start(f32[16,128,128]{2,1,0:T(8,128)S(1)} %pad_maximum_fusion), channel_id=1, source_target_pairs={{0,8},{1,9},{2,10},{3,11},{4,12},{5,13},{6,14},{7,15},{8,0},{9,1},... | collective-permute-start | bytes 3145736 | tf_op jit(solution)/shard_map/ppermute | solution.py:63
  107.8 2.9 %copy-start.1 = (f32[2,128,384]{2,1,0:T(8,128)S(1)}, f32[2,128,384]{2,1,0:T(8,128)}, u32[]{:S(2)}) copy-start(f32[2,128,384]{2,1,0:T(8,128)} %copy.54) | copy-start | bytes 1179652
  109.5 2.6 %copy-start = (f32[384,384]{1,0:T(8,128)S(1)}, f32[384,384]{1,0:T(8,128)}, u32[]{:S(2)}) copy-start(f32[384,384]{1,0:T(8,128)} %get-tuple-element.21) | copy-start | bytes 1769476
  124.9 2.5 %copy-start.4 = (f32[384,128]{1,0:T(8,128)S(1)}, f32[384,128]{1,0:T(8,128)}, u32[]{:S(2)}) copy-start(f32[384,128]{1,0:T(8,128)} %slice_select_fusion) | copy-start | bytes 589828
  127.4 1.2 copy-start.3
  128.6 1.2 copy-start.5
Sparse Core Ops, SparseCore 0:
  130.8 46.8 all-gather.1
